TPU v7x, 32 devices: a whole 2x2x4 slice. The times are simulated.
32 devices in a mesh: dp: 4 (over x, core), hidden: 4 (over z), mp: 2 (over y).
Axes of the slice: x: 2, y: 2, z: 4, core: 2. Of those that a mesh axis runs over, the one named last changes fastest.
Arguments:
- activations: bfloat16 [2048, 26624], P('dp', 'hidden'), may hold values from -6 to 6
- weight: bfloat16 [26624, 8192], P('hidden', 'mp'), may hold values from -0.0390625 to 0.0390625
- out_grad: bfloat16 [2048, 8192], P(('dp', 'hidden'), 'mp'), may hold values from -0.3125 to 0.3125
- momentum: float32 [4, 6656, 8192], P('dp', 'hidden', 'mp'), may hold values from -6 to 6
Outputs:
- output: bfloat16 [2048, 8192], P(('dp', 'hidden'), 'mp')
- new_momentum: float32 [4, 6656, 8192], P('dp', 'hidden', 'mp')
- new_weight: bfloat16 [4, 6656, 8192], P('dp', 'hidden', 'mp')
All inputs are finite; a program needn't handle non-finite values.
Results may differ from a plain program's by a relative error of at most 0.015.
Values may be sent and summed in bfloat16 or wider, within the bound.
A program may use at most 256 MiB of HBM per device.

v0:
```python
import jax
import jax.numpy as jnp
from jax import lax
from jax.sharding import PartitionSpec as P

momentum_decay = 0.9
step_size = 0.05


def on_device(activations, weight, out_grad, momentum):
    slab_rows = momentum.shape[1]
    act_rows = activations
    summed = lax.psum_scatter(
        jnp.dot(act_rows, weight, preferred_element_type=jnp.float32).astype(jnp.bfloat16),
        "hidden",
        scatter_dimension=0,
        tiled=True,
    )
    act_rows = activations
    local_grad = lax.dot_general(
        act_rows,
        lax.all_gather(out_grad, "hidden", axis=0, tiled=True),
        (((0,), (0,)), ((), ())),
        preferred_element_type=jnp.float32,
    )
    grad_share = lax.psum_scatter(
        local_grad.astype(jnp.bfloat16), "dp", scatter_dimension=0, tiled=True
    ).astype(jnp.float32)
    new_momentum = momentum_decay * momentum + grad_share[None]
    own_rows = lax.dynamic_slice_in_dim(weight, lax.axis_index("dp") * slab_rows, slab_rows, 0)
    new_weight = (own_rows.astype(jnp.float32)[None] - step_size * new_momentum).astype(
        jnp.bfloat16
    )
    return (summed, new_momentum, new_weight)


def solution(mesh):
    placed = (
        P("dp", "hidden"),
        P("hidden", "mp"),
        P(("dp", "hidden"), "mp"),
        P("dp", "hidden", "mp"),
    )
    return jax.shard_map(
        on_device,
        mesh=mesh,
        in_specs=placed,
        out_specs=(P(("dp", "hidden"), "mp"), P("dp", "hidden", "mp"), P("dp", "hidden", "mp")),
        check_vma=False,
    )
```

profile of v0, /device:TPU:0, one launch (start us, length us, event | category | flops | bytes accessed | tf_op | source)
XLA Modules:
  0.0 585.5 jit_solution(6539317287996759549)
XLA Ops:
  7.2 0.0 all-gather.2.cloned.1.call-start
  7.2 0.7 all-gather.2.cloned.1.call-update
  7.9 0.0 reduce-scatter.5.cloned.1.call-start
  7.9 85.1 %all-gather.2.cloned.1.call-done = bf16[512,4096]{1,0:T(8,128)(2,1)} async-done(((bf16[128,4096]{1,0:T(8,128)(2,1)}), bf16[512,4096]{1,0:T(8,128)(2,1)}) %all-gather.2.cloned.1.call-update) | async-done | bytes 4194320 | tf_op jit(solution)/shard_map/all_gather | solution.py:22
  93.1 37.0 %convolution_convert_fusion = bf16[6656,4096]{1,0:T(8,128)(2,1)} fusion(bf16[512,6656]{1,0:T(8,128)(2,1)} %param.4, bf16[512,4096]{1,0:T(8,128)(2,1)} %all-gather.2.cloned.1.call-done), kind=kOutput, calls=%fused_computation | convolution fusion | flops 27944550400 | bytes 65536000 | tf_op jit(solution)/shard_map/dot_general | solution.py:20
  130.1 0.0 reduce-scatter.5.cloned.1.call-update
  130.1 0.0 reduce-scatter.3.cloned.1.call-start
  130.1 40.6 %convolution_convert_fusion.1 = bf16[512,4096]{1,0:T(8,128)(2,1)} fusion(bf16[512,6656]{1,0:T(8,128)(2,1)} %param.4, bf16[6656,4096]{1,0:T(8,128)(2,1)} %param.5), kind=kOutput, calls=%fused_computation.4 | convolution fusion | flops 27919384576 | bytes 65536000 | tf_op jit(solution)/shard_map/dot_general | solution.py:14
  170.7 0.0 reduce-scatter.3.cloned.1.call-update
  170.7 328.4 %reduce-scatter.5.cloned.1.call-done = bf16[1664,4096]{1,0:T(8,128)(2,1)} async-done(((bf16[6656,4096]{1,0:T(8,128)(2,1)}), bf16[1664,4096]{1,0:T(8,128)(2,1)}) %reduce-scatter.5.cloned.1.call-update) | async-done | bytes 13631504 | tf_op jit(solution)/shard_map/reduce_scatter | solution.py:26
  499.2 32.7 %fusion = (bf16[1,1664,4096]{2,1,0:T(8,128)(2,1)}, f32[1,1664,4096]{2,1,0:T(8,128)}) fusion(bf16[6656,4096]{1,0:T(8,128)(2,1)} %param.5, s32[]{:T(128)S(6)} %select_n.3, bf16[1664,4096]{1,0:T(8,128)(2,1)} %reduce-scatter.5.cloned.1.call-done, f32[1,1664,4096]{2,1,0:T(8,128)} %param.7), kind=kLoop, calls=%fused_computation.2 | loop fusion | flops 47710208 | bytes 95420416 | tf_op jit(solution)/shard_map/convert_element_type | solution.py:31
  531.8 47.1 %reduce-scatter.3.cloned.1.call-done = bf16[128,4096]{1,0:T(8,128)(2,1)} async-done(((bf16[512,4096]{1,0:T(8,128)(2,1)}), bf16[128,4096]{1,0:T(8,128)(2,1)}) %reduce-scatter.3.cloned.1.call-update) | async-done | bytes 1048592 | tf_op jit(solution)/shard_map/reduce_scatter | solution.py:13
Async XLA Ops:
  7.2 85.9 %all-gather.2.cloned.1.call-start = ((), (), s32[]{:S(2)}) async-start(), calls=%async_computation.3 | async-start | bytes 5242880 | tf_op jit(solution)/shard_map/all_gather | solution.py:22
  7.9 491.3 %reduce-scatter.5.cloned.1.call-start = ((), (), s32[]{:S(2)}) async-start(), calls=%async_computation.4 | async-start | bytes 68157440 | tf_op jit(solution)/shard_map/reduce_scatter | solution.py:26
  130.1 448.9 %reduce-scatter.3.cloned.1.call-start = ((), (), s32[]{:S(2)}) async-start(), calls=%async_computation.2 | async-start | bytes 5242880 | tf_op jit(solution)/shard_map/reduce_scatter | solution.py:13
Sparse Core Ops, SparseCore 0:
  9.6 83.4 all-gather.1
  130.2 368.9 reduce-scatter.4
  502.1 76.7 reduce-scatter.2
where the time goes:
time: 586 us; the launch traced here: 585 us
  waiting for transfers between devices  461 us (79%)
  matrix products  77.6 us (13%)
  other arithmetic  32.7 us (6%)
  between operations  13.7 us (2%)
    reduce_scatter x1, waiting for transfers between devices, on_device(): lax.psum_scatter(local_grad.astype(jnp.bfloat16), 'dp', scatter_dimension...  328 us
    all_gather x1, waiting for transfers between devices, on_device(): lax.all_gather(out_grad, 'hidden', axis=0, tiled=True)  85.1 us
    reduce_scatter x1, waiting for transfers between devices, on_device(): lax.psum_scatter(jnp.dot(act_rows, weight, preferred_element_type=jnp.flo...  47.1 us
    dot_general x1, matrix products, on_device(): jnp.dot(act_rows, weight, preferred_element_type=jnp.float32)  40.6 us
    dot_general x1, matrix products, on_device(): lax.dot_general(act_rows, lax.all_gather(out_grad, 'hidden', axis=0, tile...  37 us
    convert_element_type x1, other arithmetic, on_device(): (own_rows.astype(jnp.float32)[None] - step_size * new_momentum).astype(jn...  32.7 us
  transfers between devices with their start and end apart: 3, of which 3 were waited for; matrix products, arithmetic and copies ran while one was open for 13% of the time, Pallas kernels for 0%

commit v1 on v0

v1 whole, which is shorter than its diff:
```python
import functools

import jax
import jax.numpy as jnp
from jax import lax
from jax.sharding import PartitionSpec as P

momentum_decay = 0.9
step_size = 0.05
parts = 2


def on_device(n_dp, n_hidden, activations, weight, out_grad, momentum):
    slab_rows = momentum.shape[1]
    me = lax.axis_index("dp")
    rows = out_grad.shape[0] // parts

    group_grad = [
        lax.all_gather(out_grad[h * rows:(h + 1) * rows], "hidden", axis=0, tiled=True)
        for h in range(parts)
    ]

    def columns_for(target):
        block = lax.dynamic_slice_in_dim(activations, target * slab_rows, slab_rows, 1)
        block = block.reshape(n_hidden, parts, rows, slab_rows)
        return block.transpose(1, 0, 2, 3).reshape(parts, n_hidden * rows, slab_rows)

    acts = {}
    for shift in range(n_dp // 2):
        for flip in range(2):
            if shift == 0 and flip == 0:
                acts[shift, flip] = columns_for(me)
                continue
            target = lax.rem((me ^ flip) + 2 * shift, n_dp)
            acts[shift, flip] = lax.ppermute(
                columns_for(target),
                "dp",
                [(j, ((j ^ flip) + 2 * shift) % n_dp) for j in range(n_dp)],
            )

    summed = lax.psum_scatter(
        jnp.dot(activations, weight, preferred_element_type=jnp.float32).astype(jnp.bfloat16),
        "hidden",
        scatter_dimension=0,
        tiled=True,
    )

    swap = [(j, j ^ 1) for j in range(n_dp)]
    total = momentum_decay * momentum[0]
    for shift in range(n_dp // 2):
        for h in range(parts):
            near = group_grad[h]
            if shift:
                near = lax.ppermute(
                    near, "dp", [(j, (j + 2 * shift) % n_dp) for j in range(n_dp)]
                )
                near, total = lax.optimization_barrier((near, total))
            far = lax.ppermute(near, "dp", swap)
            total = total + lax.dot_general(
                jnp.concatenate([acts[shift, 0][h], acts[shift, 1][h]], axis=0),
                jnp.concatenate([near, far], axis=0),
                (((0,), (0,)), ((), ())),
                preferred_element_type=jnp.float32,
            )
    new_momentum = total[None]
    own_rows = lax.dynamic_slice_in_dim(weight, me * slab_rows, slab_rows, 0)
    new_weight = (own_rows.astype(jnp.float32)[None] - step_size * new_momentum).astype(
        jnp.bfloat16
    )
    return (summed, new_momentum, new_weight)


def solution(mesh):
    placed = (
        P("dp", "hidden"),
        P("hidden", "mp"),
        P(("dp", "hidden"), "mp"),
        P("dp", "hidden", "mp"),
    )
    return jax.shard_map(
        functools.partial(on_device, mesh.shape["dp"], mesh.shape["hidden"]),
        mesh=mesh,
        in_specs=placed,
        out_specs=(P(("dp", "hidden"), "mp"), P("dp", "hidden", "mp"), P("dp", "hidden", "mp")),
        check_vma=False,
    )
```

time: 586 us -> 331 us (0.56)
  waiting for transfers between devices: 461 us -> 119 us
  matrix products: 77.6 us -> 111 us
  other arithmetic: 32.7 us -> 64.3 us
  local copies, waits for them, and re-layouts: 0 us -> 17.1 us
    reduce_scatter x2 -> x1, waiting for transfers between devices: 376 us -> 0.01 us  [on_device(): lax.psum_scatter(jnp.dot(activations, weight, preferred_element_type=jnp....]
    ppermute x0 -> x9, waiting for transfers between devices: none -> 35.6 us  [the longest x2 31.2 us: on_device(): lax.ppermute(near, 'dp', [(j, (j + 2 * shift) % n_dp) for j in range(n_dp)])]
    dot_general x2 -> x5, matrix products: 77.6 us -> 111 us  [the longest x4 74.8 us: on_device(): lax.dot_general(jnp.concatenate([acts[shift, 0][h], acts[shift, 1][h]], a...]
    add x0 -> x1, other arithmetic: none -> 27.2 us  [on_device(): total + lax.dot_general(jnp.concatenate([acts[shift, 0][h], acts[shift, 1...]
    all_gather x1 -> x2, waiting for transfers between devices: 85.1 us -> 82.3 us  [on_device(): lax.all_gather(out_grad[h * rows:(h + 1) * rows], 'hidden', axis=0, tiled...]
  transfers between devices with their start and end apart: 3 -> 12, of which waited for: 3 -> 5; matrix products, arithmetic and copies ran while one was open for 13% -> 58% of each run, Pallas kernels for 0% -> 0%
where the time goes in v1:
time: 331 us
  waiting for transfers between devices  119 us (36%)
  matrix products  111 us (34%)
  other arithmetic  64.3 us (19%)
  local copies, waits for them, and re-layouts  17.1 us (5%)
  between operations  13.8 us (4%)
  starting transfers between devices  5.57 us (2%)
    all_gather x2, waiting for transfers between devices, on_device(): lax.all_gather(out_grad[h * rows:(h + 1) * rows], 'hidden', axis=0, tiled...  82.3 us
    dot_general x4, matrix products, on_device(): lax.dot_general(jnp.concatenate([acts[shift, 0][h], acts[shift, 1][h]], a...  74.8 us
    convert_element_type x1, other arithmetic, on_device(): (own_rows.astype(jnp.float32)[None] - step_size * new_momentum).astype(jn...  37.1 us
    dot_general x1, matrix products, on_device(): jnp.dot(activations, weight, preferred_element_type=jnp.float32)  36.6 us
    ppermute x2, waiting for transfers between devices, on_device(): lax.ppermute(near, 'dp', [(j, (j + 2 * shift) % n_dp) for j in range(n_dp)])  31.2 us
    add x1, other arithmetic, on_device(): total + lax.dot_general(jnp.concatenate([acts[shift, 0][h], acts[shift, 1...  27.2 us
  transfers between devices with their start and end apart: 12, of which 5 were waited for; matrix products, arithmetic and copies ran while one was open for 58% of the time, Pallas kernels for 0%

profile of v1, /device:TPU:0, one launch (start us, length us, event | category | flops | bytes accessed | tf_op | source)
XLA Modules:
  0.0 330.8 jit_solution(11393525215453187907)
XLA Ops:
  7.2 2.3 fusion.37
  9.5 0.7 all-gather.3.cloned.1.call-update
  10.3 4.7 %constant_dynamic-slice_fusion.1 = (bf16[512,1664]{1,0:T(8,128)(2,1)}, bf16[512,1664]{1,0:T(8,128)(2,1)S(1)}, bf16[512,1664]{1,0:T(8,128)(2,1)S(1)}, bf16[512,1664]{1,0:T(8,128)(2,1)S(1)}) fusion(bf16[512,6656]{1,0:T(8,128)(2,1)} %param.4, s32[]{:T(128)S(6)} %select_n.15, s32[]{:T(128)S(6)} %select_n.14, s32[]{:T(128)S(6)} %select_n.13, s32[]{:T(128)S(6)} %select_n.16), kind=kLoop, calls=%fused_computation.41 | loop fusion | bytes 13631504 | tf_op jit(solution)/shard_map/dynamic_slice | solution.py:24
  15.0 1.3 copy.7
  16.4 0.5 collective-permute-start.2
  16.8 42.0 %all-gather.5.cloned.1.call-done = bf16[256,4096]{1,0:T(8,128)(2,1)} async-done(((bf16[64,4096]{1,0:T(8,128)(2,1)}), bf16[256,4096]{1,0:T(8,128)(2,1)}) %all-gather.5.cloned.1.call-update) | async-done | bytes 2097168 | tf_op jit(solution)/shard_map/all_gather | solution.py:19
  58.8 2.8 copy.8
  61.6 1.5 collective-permute-start.5
  63.0 1.3 copy.9
  64.8 40.3 %all-gather.3.cloned.1.call-done = bf16[256,4096]{1,0:T(8,128)(2,1)} async-done(((bf16[64,4096]{1,0:T(8,128)(2,1)}), bf16[256,4096]{1,0:T(8,128)(2,1)}) %all-gather.3.cloned.1.call-update) | async-done | bytes 2097168 | tf_op jit(solution)/shard_map/all_gather | solution.py:19
  105.2 1.5 slice_bitcast_fusion.4
  106.8 1.5 collective-permute-start.1
  108.3 16.2 %fusion.2 = f32[1664,4096]{1,0:T(8,128)} fusion(bf16[256,4096]{1,0:T(8,128)(2,1)} %collective-permute-done.3, bf16[256,4096]{1,0:T(8,128)(2,1)} %all-gather.5.cloned.1.call-done, bf16[256,1664]{1,0:T(8,128)(2,1)S(1)} %get-tuple-element.24, bf16[256,1664]{1,0:T(8,128)(2,1)S(1)} %bitcast.44), kind=kOutput, calls=%fused_computation.6 | convolution fusion | flops 6991118336 | bytes 33161216 | tf_op jit(solution)/shard_map/dot_general | solution.py:59
  124.5 27.5 %fusion = f32[1664,4096]{1,0:T(8,128)} fusion(f32[1664,4096]{1,0:T(8,128)} %fusion.2, f32[1,1664,4096]{2,1,0:T(8,128)} %param.7, bf16[256,4096]{1,0:T(8,128)(2,1)} %collective-permute-done.4, bf16[256,4096]{1,0:T(8,128)(2,1)S(1)} %copy-done, bf16[256,1664]{1,0:T(8,128)(2,1)S(1)} %get-tuple-element.23, bf16[256,1664]{1,0:T(8,128)(2,1)S(1)} %bitcast.43), kind=kOutput, calls=%fused_computation.1 | convolution fusion | flops 7011565568 | bytes 87687168 | tf_op jit(solution)/shard_map/dot_general | solution.py:59
  152.0 30.9 %collective-permute-done.1 = bf16[256,4096]{1,0:T(8,128)(2,1)} collective-permute-done((bf16[256,4096]{1,0:T(8,128)(2,1)}, bf16[256,4096]{1,0:T(8,128)(2,1)}, u32[]{:S(2)}, u32[]{:S(2)}) %collective-permute-start.1) | collective-permute-done | bytes 2097184 | tf_op jit(solution)/shard_map/ppermute | solution.py:54
  183.0 36.6 %convolution_convert_fusion = bf16[512,4096]{1,0:T(8,128)(2,1)} fusion(bf16[512,6656]{1,0:T(8,128)(2,1)} %param.4, bf16[6656,4096]{1,0:T(8,128)(2,1)} %param.5), kind=kOutput, calls=%fused_computation.5 | convolution fusion | flops 27919384576 | bytes 65536000 | tf_op jit(solution)/shard_map/dot_general | solution.py:42
  219.6 1.5 collective-permute-start
  221.2 1.5 slice_bitcast_fusion.1
  222.7 1.5 slice_bitcast_fusion
  224.3 16.1 %fusion.12 = f32[1664,4096]{1,0:T(8,128)} fusion(bf16[256,4096]{1,0:T(8,128)(2,1)} %collective-permute-done.7, bf16[256,4096]{1,0:T(8,128)(2,1)} %collective-permute-done.1, bf16[256,1664]{1,0:T(8,128)(2,1)S(1)} %get-tuple-element.20, bf16[256,1664]{1,0:T(8,128)(2,1)S(1)} %get-tuple-element.18), kind=kOutput, calls=%fused_computation.14 | convolution fusion | flops 6991118336 | bytes 33161216 | tf_op jit(solution)/shard_map/dot_general | solution.py:59
  240.4 27.2 %add.41 = f32[1664,4096]{1,0:T(8,128)} add(f32[1664,4096]{1,0:T(8,128)} %fusion, f32[1664,4096]{1,0:T(8,128)} %fusion.12) | non-fusion elementwise | flops 6815744 | bytes 81788928 | tf_op jit(solution)/shard_map/add | solution.py:59
  267.9 4.3 %collective-permute-done.8 = bf16[256,4096]{1,0:T(8,128)(2,1)S(1)} collective-permute-done((bf16[256,4096]{1,0:T(8,128)(2,1)}, bf16[256,4096]{1,0:T(8,128)(2,1)S(1)}, u32[]{:S(2)}, u32[]{:S(2)}) %collective-permute-start.8) | collective-permute-done | bytes 2097184 | tf_op jit(solution)/shard_map/ppermute | solution.py:58
  272.2 14.9 %fusion.16 = f32[1664,4096]{1,0:T(8,128)} fusion(bf16[256,4096]{1,0:T(8,128)(2,1)S(1)} %collective-permute-done.8, bf16[256,4096]{1,0:T(8,128)(2,1)} %collective-permute-done, bf16[256,1664]{1,0:T(8,128)(2,1)S(1)} %get-tuple-element.19, bf16[256,1664]{1,0:T(8,128)(2,1)S(1)} %get-tuple-element.17), kind=kOutput, calls=%fused_computation.18 | convolution fusion | flops 6991118336 | bytes 33161216 | tf_op jit(solution)/shard_map/dot_general | solution.py:59
  287.2 37.1 %fusion.1 = (bf16[1,1664,4096]{2,1,0:T(8,128)(2,1)}, f32[1,1664,4096]{2,1,0:T(8,128)}) fusion(bf16[6656,4096]{1,0:T(8,128)(2,1)} %param.5, s32[]{:T(128)S(6)} %select_n.13, f32[1664,4096]{1,0:T(8,128)} %add.41, f32[1664,4096]{1,0:T(8,128)} %fusion.16), kind=kLoop, calls=%fused_computation.3 | loop fusion | flops 34078720 | bytes 109051904 | tf_op jit(solution)/shard_map/convert_element_type | solution.py:67
  (21 shorter events, 1.1 us)
Async XLA Ops:
  7.2 51.6 %all-gather.5.cloned.1.call-start = ((), (), s32[]{:S(2)}) async-start(), calls=%async_computation.3 | async-start | bytes 2621440 | tf_op jit(solution)/shard_map/all_gather | solution.py:19
  9.5 95.6 %all-gather.3.cloned.1.call-start = ((), (), s32[]{:S(2)}) async-start(), calls=%async_computation.2 | async-start | bytes 2621440 | tf_op jit(solution)/shard_map/all_gather | solution.py:19
  10.2 314.1 %reduce-scatter.2.cloned.1.call-start = ((), (), s32[]{:S(2)}) async-start(), calls=%async_computation.1 | async-start | bytes 5242880 | tf_op jit(solution)/shard_map/reduce_scatter | solution.py:41
  16.4 88.8 %collective-permute-start.2 = (bf16[2,256,1664]{2,1,0:T(8,128)(2,1)}, bf16[2,256,1664]{2,1,0:T(8,128)(2,1)}, u32[]{:S(2)}, u32[]{:S(2)}) collective-permute-start(bf16[2,256,1664]{2,1,0:T(8,128)(2,1)} %bitcast.6), channel_id=1, source_target_pairs={{0,8},{8,0},{16,24},{24,16},{1,9},{9,1},{17,25},{25,17},{2,10},{10... | collective-permute-start | bytes 5111816 | tf_op jit(solution)/shard_map/ppermute | solution.py:35
  58.8 49.5 %collective-permute-start.3 = (bf16[256,4096]{1,0:T(8,128)(2,1)}, bf16[256,4096]{1,0:T(8,128)(2,1)}, u32[]{:S(2)}, u32[]{:S(2)}) collective-permute-start(bf16[256,4096]{1,0:T(8,128)(2,1)} %all-gather.5.cloned.1.call-done), channel_id=1, source_target_pairs={{0,8},{8,0},{16,24},{24,16},{1,9},{9,1},{17,25},{25,17},{2,10},{10... | collective-permute-start | bytes 6291464 | tf_op jit(solution)/shard_map/ppermute | solution.py:58
  61.6 159.6 %collective-permute-start.5 = (bf16[2,256,1664]{2,1,0:T(8,128)(2,1)}, bf16[2,256,1664]{2,1,0:T(8,128)(2,1)}, u32[]{:S(2)}, u32[]{:S(2)}) collective-permute-start(bf16[2,256,1664]{2,1,0:T(8,128)(2,1)} %bitcast.13), channel_id=1, source_target_pairs={{0,16},{8,24},{16,0},{24,8},{1,17},{9,25},{17,1},{25,9},{2,18},{10... | collective-permute-start | bytes 5111816 | tf_op jit(solution)/shard_map/ppermute | solution.py:35
  64.4 158.3 %collective-permute-start.6 = (bf16[2,256,1664]{2,1,0:T(8,128)(2,1)}, bf16[2,256,1664]{2,1,0:T(8,128)(2,1)}, u32[]{:S(2)}, u32[]{:S(2)}) collective-permute-start(bf16[2,256,1664]{2,1,0:T(8,128)(2,1)} %bitcast.17), channel_id=1, source_target_pairs={{0,24},{8,16},{16,8},{24,0},{1,25},{9,17},{17,9},{25,1},{2,26},{10... | collective-permute-start | bytes 5111816 | tf_op jit(solution)/shard_map/ppermute | solution.py:35
  105.1 19.4 %collective-permute-start.4 = (bf16[256,4096]{1,0:T(8,128)(2,1)}, bf16[256,4096]{1,0:T(8,128)(2,1)}, u32[]{:S(2)}, u32[]{:S(2)}) collective-permute-start(bf16[256,4096]{1,0:T(8,128)(2,1)} %all-gather.3.cloned.1.call-done), channel_id=1, source_target_pairs={{0,8},{8,0},{16,24},{24,16},{1,9},{9,1},{17,25},{25,17},{2,10},{10... | collective-permute-start | bytes 6291464 | tf_op jit(solution)/shard_map/ppermute | solution.py:58
  106.8 76.2 %collective-permute-start.1 = (bf16[256,4096]{1,0:T(8,128)(2,1)}, bf16[256,4096]{1,0:T(8,128)(2,1)}, u32[]{:S(2)}, u32[]{:S(2)}) collective-permute-start(bf16[256,4096]{1,0:T(8,128)(2,1)} %all-gather.5.cloned.1.call-done), channel_id=1, source_target_pairs={{0,16},{8,24},{16,0},{24,8},{1,17},{9,25},{17,1},{25,9},{2,18},{10... | collective-permute-start | bytes 6291464 | tf_op jit(solution)/shard_map/ppermute | solution.py:54
  108.3 16.2 %copy-start = (bf16[256,4096]{1,0:T(8,128)(2,1)S(1)}, bf16[256,4096]{1,0:T(8,128)(2,1)}, u32[]{:S(2)}) copy-start(bf16[256,4096]{1,0:T(8,128)(2,1)} %all-gather.3.cloned.1.call-done) | copy-start | bytes 6291460
  183.0 41.3 %collective-permute-start.7 = (bf16[256,4096]{1,0:T(8,128)(2,1)}, bf16[256,4096]{1,0:T(8,128)(2,1)}, u32[]{:S(2)}, u32[]{:S(2)}) collective-permute-start(bf16[256,4096]{1,0:T(8,128)(2,1)} %collective-permute-done.1), channel_id=1, source_target_pairs={{0,8},{8,0},{16,24},{24,16},{1,9},{9,1},{17,25},{25,17},{2,10},{10... | collective-permute-start | bytes 6291464 | tf_op jit(solution)/shard_map/ppermute | solution.py:58
  219.6 48.2 %collective-permute-start = (bf16[256,4096]{1,0:T(8,128)(2,1)S(1)}, bf16[256,4096]{1,0:T(8,128)(2,1)}, u32[]{:S(2)}, u32[]{:S(2)}) collective-permute-start(bf16[256,4096]{1,0:T(8,128)(2,1)S(1)} %copy-done), channel_id=1, source_target_pairs={{0,16},{8,24},{16,0},{24,8},{1,17},{9,25},{17,1},{25,9},{2,18},{10... | collective-permute-start | bytes 6291464 | tf_op jit(solution)/shard_map/ppermute | solution.py:54
  267.9 4.4 %collective-permute-start.8 = (bf16[256,4096]{1,0:T(8,128)(2,1)}, bf16[256,4096]{1,0:T(8,128)(2,1)S(1)}, u32[]{:S(2)}, u32[]{:S(2)}) collective-permute-start(bf16[256,4096]{1,0:T(8,128)(2,1)} %collective-permute-done), channel_id=1, source_target_pairs={{0,8},{8,0},{16,24},{24,16},{1,9},{9,1},{17,25},{25,17},{2,10},{10... | collective-permute-start | bytes 6291464 | tf_op jit(solution)/shard_map/ppermute | solution.py:58
Sparse Core Ops, SparseCore 0:
  10.1 48.6 all-gather.4
  60.4 44.6 all-gather.2
  219.8 75.6 reduce-scatter.1

commit v2 on v1

v2 whole, which is shorter than its diff:
```python
import functools

import jax
import jax.numpy as jnp
from jax import lax
from jax.sharding import PartitionSpec as P

momentum_decay = 0.9
step_size = 0.05
parts = 2


def on_device(n_dp, n_hidden, activations, weight, out_grad, momentum):
    slab_rows = momentum.shape[1]
    me = lax.axis_index("dp")
    rows = out_grad.shape[0] // parts

    group_grad = [
        lax.all_gather(out_grad[h * rows:(h + 1) * rows], "hidden", axis=0, tiled=True)
        for h in range(parts)
    ]

    def columns_for(target):
        block = lax.dynamic_slice_in_dim(activations, target * slab_rows, slab_rows, 1)
        block = block.reshape(n_hidden, parts, rows, slab_rows)
        return block.transpose(1, 0, 2, 3).reshape(parts, n_hidden * rows, slab_rows)

    blocks = {
        (shift, flip): columns_for(lax.rem((me ^ flip) + 2 * shift, n_dp))
        for shift in range(n_dp // 2)
        for flip in range(2)
    }
    blocks, act_rows = lax.optimization_barrier((blocks, activations))
    acts = {
        (shift, flip): lax.ppermute(
            block, "dp", [(j, ((j ^ flip) + 2 * shift) % n_dp) for j in range(n_dp)]
        )
        if shift or flip
        else block
        for (shift, flip), block in blocks.items()
    }

    product = jnp.dot(act_rows, weight, preferred_element_type=jnp.float32).astype(jnp.bfloat16)
    summed = lax.psum_scatter(product, "hidden", scatter_dimension=0, tiled=True)
    _, acts, group_grad[0] = lax.optimization_barrier((product, acts, group_grad[0]))

    swap = [(j, j ^ 1) for j in range(n_dp)]
    total = momentum_decay * momentum[0]
    for shift in range(n_dp // 2):
        lefts, rights = [], []
        for h in range(parts):
            near = group_grad[h]
            if shift:
                near = lax.ppermute(
                    near, "dp", [(j, (j + 2 * shift) % n_dp) for j in range(n_dp)]
                )
                if h == 0:
                    near, total = lax.optimization_barrier((near, total))
            lefts += [acts[shift, 0][h], acts[shift, 1][h]]
            rights += [near, lax.ppermute(near, "dp", swap)]
        if shift + 1 == n_dp // 2:
            summed, total = lax.optimization_barrier((summed, total))
        total = total + lax.dot_general(
            jnp.concatenate(lefts, axis=0),
            jnp.concatenate(rights, axis=0),
            (((0,), (0,)), ((), ())),
            preferred_element_type=jnp.float32,
        )
    new_momentum = total[None]
    own_rows = lax.dynamic_slice_in_dim(weight, me * slab_rows, slab_rows, 0)
    new_weight = (own_rows.astype(jnp.float32)[None] - step_size * new_momentum).astype(
        jnp.bfloat16
    )
    return (summed, new_momentum, new_weight)


def solution(mesh):
    placed = (
        P("dp", "hidden"),
        P("hidden", "mp"),
        P(("dp", "hidden"), "mp"),
        P("dp", "hidden", "mp"),
    )
    return jax.shard_map(
        functools.partial(on_device, mesh.shape["dp"], mesh.shape["hidden"]),
        mesh=mesh,
        in_specs=placed,
        out_specs=(P(("dp", "hidden"), "mp"), P("dp", "hidden", "mp"), P("dp", "hidden", "mp")),
        check_vma=False,
    )
```

time: 331 us -> 261 us (0.79)
  other arithmetic: 64.3 us -> 19.2 us
  matrix products: 111 us -> 95.8 us
  waiting for transfers between devices: 119 us -> 112 us
  local copies, waits for them, and re-layouts: 17.1 us -> 13.5 us
    all_gather x2, waiting for transfers between devices: 82.3 us -> 11.6 us  [on_device(): lax.all_gather(out_grad[h * rows:(h + 1) * rows], 'hidden', axis=0, tiled...]
    ppermute x7, waiting for transfers between devices: 4.32 us -> 44.4 us  [the longest x3 37.4 us: on_device(): lax.ppermute(block, 'dp', [(j, ((j ^ flip) + 2 * shift) % n_dp) for j in...]
    add x1 -> x0, other arithmetic: 27.2 us -> none  [on_device(): total + lax.dot_general(jnp.concatenate([acts[shift, 0][h], acts[shift, 1...]
    ppermute x2, waiting for transfers between devices: 31.2 us -> 56.2 us  [on_device(): lax.ppermute(near, 'dp', [(j, (j + 2 * shift) % n_dp) for j in range(n_dp)])]
    convert_element_type x1, other arithmetic: 37.1 us -> 19.2 us  [on_device(): (own_rows.astype(jnp.float32)[None] - step_size * new_momentum).astype(jn...]
    dot_general x5 -> x3, matrix products: 111 us -> 95.8 us  [the longest x2 58.9 us: on_device(): lax.dot_general(jnp.concatenate(lefts, axis=0), jnp.concatenate(rights, a...]
  transfers between devices with their start and end apart: 12 -> 12, of which waited for: 5 -> 8; matrix products, arithmetic and copies ran while one was open for 58% -> 30% of each run, Pallas kernels for 0% -> 0%
where the time goes in v2:
time: 261 us
  waiting for transfers between devices  112 us (43%)
  matrix products  95.8 us (37%)
  other arithmetic  19.2 us (7%)
  between operations  13.8 us (5%)
  local copies, waits for them, and re-layouts  13.5 us (5%)
  starting transfers between devices  6.38 us (2%)
    dot_general x2, matrix products, on_device(): lax.dot_general(jnp.concatenate(lefts, axis=0), jnp.concatenate(rights, a...  58.9 us
    ppermute x2, waiting for transfers between devices, on_device(): lax.ppermute(near, 'dp', [(j, (j + 2 * shift) % n_dp) for j in range(n_dp)])  56.2 us
    ppermute x3, waiting for transfers between devices, on_device(): lax.ppermute(block, 'dp', [(j, ((j ^ flip) + 2 * shift) % n_dp) for j in...  37.4 us
    dot_general x1, matrix products, on_device(): jnp.dot(act_rows, weight, preferred_element_type=jnp.float32)  36.9 us
    convert_element_type x1, other arithmetic, on_device(): (own_rows.astype(jnp.float32)[None] - step_size * new_momentum).astype(jn...  19.2 us
    all_gather x2, waiting for transfers between devices, on_device(): lax.all_gather(out_grad[h * rows:(h + 1) * rows], 'hidden', axis=0, tiled...  11.6 us
    ppermute x4, waiting for transfers between devices, on_device(): rights += [near, lax.ppermute(near, 'dp', swap)]  7.03 us
  transfers between devices with their start and end apart: 12, of which 8 were waited for; matrix products, arithmetic and copies ran while one was open for 30% of the time, Pallas kernels for 0%

profile of v2, /device:TPU:0, one launch (start us, length us, event | category | flops | bytes accessed | tf_op | source)
XLA Modules:
  0.0 260.9 jit_solution(14794245780964217814)
XLA Ops:
  7.2 2.3 fusion.31
  9.6 3.5 %constant_dynamic-slice_fusion = (bf16[512,1664]{1,0:T(8,128)(2,1)S(1)}, bf16[512,1664]{1,0:T(8,128)(2,1)S(1)}, bf16[512,1664]{1,0:T(8,128)(2,1)S(1)}, bf16[512,1664]{1,0:T(8,128)(2,1)S(1)}) fusion(bf16[512,6656]{1,0:T(8,128)(2,1)} %param.4, s32[]{:T(128)S(6)} %select_n.18, s32[]{:T(128)S(6)} %select_n.17, s32[]{:T(128)S(6)} %select_n.16, s32[]{:T(128)S(6)} %select_n.15), kind=kLoop, calls=%fused_computation.41 | loop fusion | bytes 13631504 | tf_op jit(solution)/shard_map/dynamic_slice | solution.py:24
  13.3 1.4 copy.9
  14.6 1.3 copy.8
  16.1 0.5 collective-permute-start
  16.6 2.6 collective-permute-start.1
  19.3 36.9 %convolution_convert_fusion = bf16[512,4096]{1,0:T(8,128)(2,1)} fusion(bf16[512,6656]{1,0:T(8,128)(2,1)} %param.4, bf16[6656,4096]{1,0:T(8,128)(2,1)} %param.5), kind=kOutput, calls=%fused_computation.18 | convolution fusion | flops 27919384576 | bytes 65536000 | tf_op jit(solution)/shard_map/dot_general | solution.py:43
  56.2 1.4 collective-permute-done.1
  57.5 36.0 %collective-permute-done.2 = bf16[2,256,1664]{2,1,0:T(8,128)(2,1)} collective-permute-done((bf16[2,256,1664]{2,1,0:T(8,128)(2,1)S(1)}, bf16[2,256,1664]{2,1,0:T(8,128)(2,1)}, u32[]{:S(2)}, u32[]{:S(2)}) %collective-permute-start.2) | collective-permute-done | bytes 1703968 | tf_op jit(solution)/shard_map/ppermute | solution.py:35
  93.5 11.6 %all-gather.5.cloned.1.call-done = bf16[256,4096]{1,0:T(8,128)(2,1)} async-done(((bf16[64,4096]{1,0:T(8,128)(2,1)}), bf16[256,4096]{1,0:T(8,128)(2,1)}) %all-gather.5.cloned.1.call-update) | async-done | bytes 2097168 | tf_op jit(solution)/shard_map/all_gather | solution.py:19
  105.1 0.5 collective-permute-start.4
  105.7 1.5 collective-permute-start.3
  107.2 0.6 collective-permute-start.7
  107.7 2.6 %slice_bitcast_fusion.6 = (bf16[256,1664]{1,0:T(8,128)(2,1)S(1)}, bf16[256,1664]{1,0:T(8,128)(2,1)S(1)}, bf16[256,1664]{1,0:T(8,128)(2,1)S(1)}, bf16[256,1664]{1,0:T(8,128)(2,1)}) fusion(bf16[2,256,1664]{2,1,0:T(8,128)(2,1)} %collective-permute-done, bf16[2,256,1664]{2,1,0:T(8,128)(2,1)S(1)} %bitcast.44), kind=kLoop, calls=%fused_computation.39 | loop fusion | bytes 6815744 | tf_op jit(solution)/shard_map/squeeze | solution.py:59
  110.4 2.2 collective-permute-done.4
  112.6 29.7 %bitcast_add_fusion = f32[1664,4096]{1,0:T(8,128)} fusion(f32[1,1664,4096]{2,1,0:T(8,128)} %param.7, bf16[256,4096]{1,0:T(8,128)(2,1)} %collective-permute-done.5, bf16[256,4096]{1,0:T(8,128)(2,1)} %all-gather.5.cloned.1.call-done, bf16[256,4096]{1,0:T(8,128)(2,1)} %collective-permute-done.4, bf16[256,4096]{1,0:T(8,128)(2,1)} %all-gather.3.cloned.1.call-done, ...), kind=kOutput, calls=%fused_computation | convolution fusion | flops 14019461120 | bytes 66322432 | tf_op jit(solution)/shard_map/dot_general | solution.py:63
  142.3 12.2 %collective-permute-done.3 = bf16[256,4096]{1,0:T(8,128)(2,1)} collective-permute-done((bf16[256,4096]{1,0:T(8,128)(2,1)}, bf16[256,4096]{1,0:T(8,128)(2,1)}, u32[]{:S(2)}, u32[]{:S(2)}) %collective-permute-start.3) | collective-permute-done | bytes 2097184 | tf_op jit(solution)/shard_map/ppermute | solution.py:54
  154.5 44.0 %collective-permute-done.7 = bf16[256,4096]{1,0:T(8,128)(2,1)} collective-permute-done((bf16[256,4096]{1,0:T(8,128)(2,1)}, bf16[256,4096]{1,0:T(8,128)(2,1)}, u32[]{:S(2)}, u32[]{:S(2)}) %collective-permute-start.7) | collective-permute-done | bytes 2097184 | tf_op jit(solution)/shard_map/ppermute | solution.py:54
  198.5 0.5 collective-permute-start.6
  199.0 2.2 slice_bitcast_fusion.2
  201.2 1.8 collective-permute-done.8
  203.0 3.0 %collective-permute-done.6 = bf16[256,4096]{1,0:T(8,128)(2,1)} collective-permute-done((bf16[256,4096]{1,0:T(8,128)(2,1)}, bf16[256,4096]{1,0:T(8,128)(2,1)}, u32[]{:S(2)}, u32[]{:S(2)}) %collective-permute-start.6) | collective-permute-done | bytes 2097184 | tf_op jit(solution)/shard_map/ppermute | solution.py:60
  206.0 29.2 %convolution_add_fusion = f32[1664,4096]{1,0:T(8,128)} fusion(f32[1664,4096]{1,0:T(8,128)} %bitcast_add_fusion, bf16[256,4096]{1,0:T(8,128)(2,1)} %collective-permute-done.8, bf16[256,4096]{1,0:T(8,128)(2,1)} %collective-permute-done.7, bf16[256,4096]{1,0:T(8,128)(2,1)} %collective-permute-done.6, bf16[256,4096]{1,0:T(8,128)(2,1)} %collective-permute-done.3, ...), kind=kOutput, calls=%fused_computation.2 | convolution fusion | flops 14012645376 | bytes 66322432 | tf_op jit(solution)/shard_map/dot_general | solution.py:63
  235.2 19.2 %fusion = bf16[1,1664,4096]{2,1,0:T(8,128)(2,1)} fusion(f32[1664,4096]{1,0:T(8,128)} %convolution_add_fusion, bf16[6656,4096]{1,0:T(8,128)(2,1)} %param.5, s32[]{:T(128)S(6)} %select_n.19), kind=kLoop, calls=%fused_computation.3 | loop fusion | flops 27262976 | bytes 54525956 | tf_op jit(solution)/shard_map/convert_element_type | solution.py:71
  (15 shorter events, 0.5 us)
Async XLA Ops:
  7.2 86.4 %all-gather.3.cloned.1.call-start = ((), (), s32[]{:S(2)}) async-start(), calls=%async_computation.2 | async-start | bytes 2621440 | tf_op jit(solution)/shard_map/all_gather | solution.py:19
  9.5 95.6 %all-gather.5.cloned.1.call-start = ((), (), s32[]{:S(2)}) async-start(), calls=%async_computation.3 | async-start | bytes 2621440 | tf_op jit(solution)/shard_map/all_gather | solution.py:19
  16.1 40.1 %collective-permute-start = (bf16[2,256,1664]{2,1,0:T(8,128)(2,1)}, bf16[2,256,1664]{2,1,0:T(8,128)(2,1)}, u32[]{:S(2)}, u32[]{:S(2)}) collective-permute-start(bf16[2,256,1664]{2,1,0:T(8,128)(2,1)} %bitcast.5), channel_id=1, source_target_pairs={{0,8},{8,0},{16,24},{24,16},{1,9},{9,1},{17,25},{25,17},{2,10},{10... | collective-permute-start | bytes 5111816 | tf_op jit(solution)/shard_map/ppermute | solution.py:35
  16.6 40.9 %collective-permute-start.1 = (bf16[2,256,1664]{2,1,0:T(8,128)(2,1)}, bf16[2,256,1664]{2,1,0:T(8,128)(2,1)}, u32[]{:S(2)}, u32[]{:S(2)}) collective-permute-start(bf16[2,256,1664]{2,1,0:T(8,128)(2,1)} %bitcast.8), channel_id=1, source_target_pairs={{0,16},{8,24},{16,0},{24,8},{1,17},{9,25},{17,1},{25,9},{2,18},{10... | collective-permute-start | bytes 5111816 | tf_op jit(solution)/shard_map/ppermute | solution.py:35
  19.2 74.4 %collective-permute-start.2 = (bf16[2,256,1664]{2,1,0:T(8,128)(2,1)S(1)}, bf16[2,256,1664]{2,1,0:T(8,128)(2,1)}, u32[]{:S(2)}, u32[]{:S(2)}) collective-permute-start(bf16[2,256,1664]{2,1,0:T(8,128)(2,1)S(1)} %bitcast.45), channel_id=1, source_target_pairs={{0,24},{8,16},{16,8},{24,0},{1,25},{9,17},{17,9},{25,1},{2,26},{10... | collective-permute-start | bytes 5111816 | tf_op jit(solution)/shard_map/ppermute | solution.py:35
  19.3 182.0 %reduce-scatter.2.cloned.1.call-start = ((), (), s32[]{:S(2)}) async-start(), calls=%async_computation.1 | async-start | bytes 5242880 | tf_op jit(solution)/shard_map/reduce_scatter | solution.py:44
  105.1 5.3 %collective-permute-start.5 = (bf16[256,4096]{1,0:T(8,128)(2,1)}, bf16[256,4096]{1,0:T(8,128)(2,1)}, u32[]{:S(2)}, u32[]{:S(2)}) collective-permute-start(bf16[256,4096]{1,0:T(8,128)(2,1)} %all-gather.5.cloned.1.call-done), channel_id=1, source_target_pairs={{0,8},{8,0},{16,24},{24,16},{1,9},{9,1},{17,25},{25,17},{2,10},{10... | collective-permute-start | bytes 6291464 | tf_op jit(solution)/shard_map/ppermute | solution.py:60
  105.1 7.5 %collective-permute-start.4 = (bf16[256,4096]{1,0:T(8,128)(2,1)}, bf16[256,4096]{1,0:T(8,128)(2,1)}, u32[]{:S(2)}, u32[]{:S(2)}) collective-permute-start(bf16[256,4096]{1,0:T(8,128)(2,1)} %all-gather.3.cloned.1.call-done), channel_id=1, source_target_pairs={{0,8},{8,0},{16,24},{24,16},{1,9},{9,1},{17,25},{25,17},{2,10},{10... | collective-permute-start | bytes 6291464 | tf_op jit(solution)/shard_map/ppermute | solution.py:60
  105.7 48.9 %collective-permute-start.3 = (bf16[256,4096]{1,0:T(8,128)(2,1)}, bf16[256,4096]{1,0:T(8,128)(2,1)}, u32[]{:S(2)}, u32[]{:S(2)}) collective-permute-start(bf16[256,4096]{1,0:T(8,128)(2,1)} %all-gather.3.cloned.1.call-done), channel_id=1, source_target_pairs={{0,16},{8,24},{16,0},{24,8},{1,17},{9,25},{17,1},{25,9},{2,18},{10... | collective-permute-start | bytes 6291464 | tf_op jit(solution)/shard_map/ppermute | solution.py:54
  107.2 91.3 %collective-permute-start.7 = (bf16[256,4096]{1,0:T(8,128)(2,1)}, bf16[256,4096]{1,0:T(8,128)(2,1)}, u32[]{:S(2)}, u32[]{:S(2)}) collective-permute-start(bf16[256,4096]{1,0:T(8,128)(2,1)} %all-gather.5.cloned.1.call-done), channel_id=1, source_target_pairs={{0,16},{8,24},{16,0},{24,8},{1,17},{9,25},{17,1},{25,9},{2,18},{10... | collective-permute-start | bytes 6291464 | tf_op jit(solution)/shard_map/ppermute | solution.py:54
  198.5 4.5 %collective-permute-start.8 = (bf16[256,4096]{1,0:T(8,128)(2,1)}, bf16[256,4096]{1,0:T(8,128)(2,1)}, u32[]{:S(2)}, u32[]{:S(2)}) collective-permute-start(bf16[256,4096]{1,0:T(8,128)(2,1)} %collective-permute-done.7), channel_id=1, source_target_pairs={{0,8},{8,0},{16,24},{24,16},{1,9},{9,1},{17,25},{25,17},{2,10},{10... | collective-permute-start | bytes 6291464 | tf_op jit(solution)/shard_map/ppermute | solution.py:60
  198.5 7.5 %collective-permute-start.6 = (bf16[256,4096]{1,0:T(8,128)(2,1)}, bf16[256,4096]{1,0:T(8,128)(2,1)}, u32[]{:S(2)}, u32[]{:S(2)}) collective-permute-start(bf16[256,4096]{1,0:T(8,128)(2,1)} %collective-permute-done.3), channel_id=1, source_target_pairs={{0,8},{8,0},{16,24},{24,16},{1,9},{9,1},{17,25},{25,17},{2,10},{10... | collective-permute-start | bytes 6291464 | tf_op jit(solution)/shard_map/ppermute | solution.py:60
Sparse Core Ops, SparseCore 0:
  9.6 48.6 all-gather.2
  60.4 44.6 all-gather.4
  108.0 75.4 reduce-scatter.1
